TPU v7x, 512 devices: a whole 4x8x8 slice. The times are simulated.
512 devices in a mesh: tm: 128 (over z, y, core), rows: 4 (over x).
Axes of the slice: x: 4, y: 8, z: 8, core: 2. Of those that a mesh axis runs over, the one named last changes fastest.
Arguments:
- pivot_blocks: float32 [128, 512, 512], P('tm'), may hold values from -4 to 24, as said below
- lower_blocks: float32 [128, 512, 512], P('tm', None, 'rows'), may hold values from -5 to 0.5
- top_diagonal: float32 [128, 512, 512], P('tm', 'rows'), may hold values from -1 to 2, as said below
- top_coupling: float32 [128, 512, 512], P('tm', 'rows'), may hold values from -3 to 3
Outputs:
- sigma_diagonal: float32 [128, 512, 512], P('tm', 'rows')
- sigma_next: float32 [128, 512, 512], P('tm', 'rows')
- reduced_pivot: float32 [128, 512, 512], P('tm', 'rows')
Inputs may be any that keep to these rules, and one draw needn't show every extreme that they name: `pivot_blocks`: each block is symmetric, and the block-tridiagonal matrix with these diagonal blocks and the couplings lower_blocks is positive definite. `top_diagonal`: each block is symmetric.
All inputs are finite; a program needn't handle non-finite values.
Results may differ from a plain program's by a relative error of at most 0.0001.
Values sent between devices are 32-bit elements; how exact they have to be, the bound alone decides.
A program may use at most 64 MiB of HBM per device.

v0:
```python
import jax
import jax.numpy as jnp
from jax import lax
from jax.sharding import PartitionSpec as P

LEVELS = 2
precise = lax.Precision.HIGHEST


def passed_along(value, axis, steps):
    count = lax.axis_size(axis)
    leading, last = (max(0, -steps), min(count, count - steps))
    return lax.ppermute(value, axis, [(source, source + steps) for source in range(leading, last)])


def product(left, right):
    return jnp.dot(left, right, precision=precise, preferred_element_type=jnp.float32)


def product_flip(left, right):
    return lax.dot_general(
        left, right, (((1,), (1,)), ((), ())), precision=precise, preferred_element_type=jnp.float32
    )


def product_over(left, right):
    return lax.dot_general(
        left, right, (((0,), (0,)), ((), ())), precision=precise, preferred_element_type=jnp.float32
    )


def solve_with(factor, right_side):
    return jax.scipy.linalg.cho_solve((factor, True), right_side)


def local(pivot_blocks, lower_blocks, top_diagonal, top_coupling):
    parts_count = lax.axis_size("tm")
    position = lax.axis_index("tm")
    row_part = lax.axis_index("rows")
    full_width = pivot_blocks.shape[1]
    quarter = lower_blocks.shape[2]
    row_start = row_part * quarter
    first_pivot = pivot_blocks[0]
    lower_columns = jnp.where(position == 0, jnp.zeros_like(lower_blocks[0]), lower_blocks[0])
    lower_rows = lax.all_to_all(lower_columns, "rows", split_axis=0, concat_axis=1, tiled=True)
    next_rows = passed_along(lower_rows, "tm", -1)
    upper_columns = next_rows.T
    pivot_rows = lax.dynamic_slice_in_dim(first_pivot, row_start, quarter, 0)
    unit_columns = (
        jnp.arange(full_width)[:, None] == row_start + jnp.arange(quarter)[None, :]
    ).astype(jnp.float32)
    saved = []
    for tier_index in range(LEVELS):
        spacing = 2**tier_index
        if tier_index == 0:
            whole_pivot = first_pivot
        else:
            whole_pivot = lax.all_gather(pivot_rows, "rows", axis=0, tiled=True)
        factor = jnp.linalg.cholesky(whole_pivot)
        solved = solve_with(
            factor, jnp.concatenate([lower_columns, upper_columns, unit_columns], axis=1)
        )
        left_columns = solved[:, :quarter]
        right_columns = solved[:, quarter : 2 * quarter]
        inverse_columns = solved[:, 2 * quarter :]
        left_solved, right_solved = (
            lax.all_gather(left_columns, "rows", axis=1, tiled=True),
            lax.all_gather(right_columns, "rows", axis=1, tiled=True),
        )
        drop_left = product_over(lower_columns, left_solved)
        upper_new = -product_over(upper_columns, left_solved)
        left_bound = passed_along(jnp.stack([drop_left, upper_new]), "tm", -spacing)
        drop_right = product_over(upper_columns, right_solved)
        lower_new = -product_over(lower_columns, right_solved)
        right_bound = passed_along(jnp.stack([drop_right, lower_new]), "tm", spacing)
        pivot_rows = pivot_rows - left_bound[0] - right_bound[0]
        upper_columns = left_bound[1].T
        lower_columns = right_bound[1].T
        saved.append((left_solved, right_solved, inverse_columns))
    diagonal_rows = top_diagonal[0]
    coupling_rows = jnp.where(
        position + 2**LEVELS >= parts_count, jnp.zeros_like(top_coupling[0]), top_coupling[0]
    )
    for tier_index in reversed(range(LEVELS)):
        spacing = 2**tier_index
        saved_left, saved_right, saved_inverse = saved[tier_index]
        left_rows = lax.dynamic_slice_in_dim(saved_left, row_start, quarter, 0)
        right_rows = lax.dynamic_slice_in_dim(saved_right, row_start, quarter, 0)
        gathered = lax.all_gather(
            jnp.stack([diagonal_rows, coupling_rows]), "rows", axis=1, tiled=True
        )
        from_left = passed_along(gathered, "tm", spacing)
        far_diagonal = passed_along(gathered[0], "tm", -spacing)
        near_diagonal = from_left[0]
        near_next = from_left[1]
        cross_near = product(left_rows, near_diagonal) + product_flip(right_rows, near_next)
        cross_far = product(left_rows, near_next) + product(right_rows, far_diagonal)
        diagonal_rows = (
            saved_inverse.T
            + product_flip(cross_near, saved_left)
            + product_flip(cross_far, saved_right)
        )
        coupling_rows = -cross_far
    coupling_rows = jnp.where(
        position == parts_count - 1, jnp.zeros_like(coupling_rows), coupling_rows
    )
    return (diagonal_rows[None], coupling_rows[None], pivot_rows[None])


def solution(mesh):
    placed = (
        P("tm", None, None),
        P("tm", None, "rows"),
        P("tm", "rows", None),
        P("tm", "rows", None),
    )
    return jax.shard_map(
        local,
        mesh=mesh,
        in_specs=placed,
        out_specs=(P("tm", "rows", None), P("tm", "rows", None), P("tm", "rows", None)),
        check_vma=False,
    )
```

profile of v0, /device:TPU:256, one launch (start us, length us, event | category | flops | bytes accessed | tf_op | source)
XLA Modules:
  0.0 630.2 jit_solution(3669851343186253407)
XLA Ops:
  14.0 11.7 %cholesky.286 = f32[128,128]{1,0:T(8,128)S(1)} custom-call(f32[128,128]{1,0:T(8,128)S(1)} %cholesky.426), custom_call_target="Cholesky" | custom-call | tf_op jit(solution)/shard_map/jit(cholesky)/cholesky | solution.py:59
  25.7 9.8 %custom-call.29 = f32[1,128,128]{1,2,0:T(8,128)S(1)} custom-call(f32[1,128,128]{2,1,0:T(8,128)S(1)} %get-tuple-element.70), custom_call_target="InvertDiagBlocksLowerTriangular" | custom-call | tf_op jit(solution)/shard_map/jit(cholesky)/cholesky | solution.py:59
  37.0 11.7 %cholesky.305 = f32[128,128]{1,0:T(8,128)S(1)} custom-call(f32[128,128]{1,0:T(8,128)S(1)} %cholesky.430), custom_call_target="Cholesky" | custom-call | tf_op jit(solution)/shard_map/jit(cholesky)/cholesky | solution.py:59
  48.8 10.2 %custom-call.30 = f32[1,128,128]{1,2,0:T(8,128)S(1)} custom-call(f32[1,128,128]{2,1,0:T(8,128)S(1)} %get-tuple-element.67), custom_call_target="InvertDiagBlocksLowerTriangular" | custom-call | tf_op jit(solution)/shard_map/jit(cholesky)/cholesky | solution.py:59
  61.2 13.2 %cholesky.326 = f32[128,128]{1,0:T(8,128)} custom-call(f32[128,128]{1,0:T(8,128)} %cholesky.435), custom_call_target="Cholesky" | custom-call | tf_op jit(solution)/shard_map/jit(cholesky)/cholesky | solution.py:59
  76.5 11.3 %custom-call.31 = f32[1,128,128]{1,2,0:T(8,128)} custom-call(f32[1,128,128]{2,1,0:T(8,128)} %get-tuple-element.64), custom_call_target="InvertDiagBlocksLowerTriangular" | custom-call | tf_op jit(solution)/shard_map/jit(cholesky)/cholesky | solution.py:59
  89.2 11.7 %cholesky.343 = f32[128,128]{1,0:T(8,128)S(1)} custom-call(f32[128,128]{1,0:T(8,128)S(1)} %convolution_subtract_fusion.14), custom_call_target="Cholesky" | custom-call | tf_op jit(solution)/shard_map/jit(cholesky)/cholesky | solution.py:59
  117.0 39.3 %custom-call.32 = f32[4,128,128]{1,2,0:T(8,128)S(1)} custom-call(f32[4,128,128]{2,1,0:T(8,128)S(1)} %get-tuple-element.19), custom_call_target="InvertDiagBlocksLowerTriangular" | custom-call | tf_op jit(solution)/shard_map/jit(_cho_solve)/triangular_solve | solution.py:33
  165.5 31.1 %all-gather.9.cloned.1.call-done = f32[512,512]{1,0:T(8,128)} async-done(((f32[512,128]{1,0:T(8,128)}), f32[512,512]{1,0:T(8,128)}) %all-gather.9.cloned.1.call-update) | async-done | bytes 1048592 | tf_op jit(solution)/shard_map/all_gather | solution.py:67
  205.5 26.0 %all-gather.11.cloned.1.call-done = f32[512,512]{1,0:T(8,128)} async-done(((f32[512,128]{1,0:T(8,128)}), f32[512,512]{1,0:T(8,128)}) %all-gather.11.cloned.1.call-update) | async-done | bytes 1048592 | tf_op jit(solution)/shard_map/all_gather | solution.py:68
  239.3 12.2 %collective-permute-done.2 = f32[2,128,512]{1,2,0:T(8,128)} collective-permute-done((f32[2,128,512]{1,2,0:T(8,128)}, f32[2,128,512]{1,2,0:T(8,128)}, u32[]{:S(2)}, u32[]{:S(2)}) %collective-permute-start.2) | collective-permute-done | bytes 524320 | tf_op jit(solution)/shard_map/ppermute | solution.py:13
  257.9 26.0 %all-gather.21.cloned.1.call-done = f32[1,512,512]{1,2,0:T(8,128)} async-done(((f32[1,128,512]{1,2,0:T(8,128)}), f32[1,512,512]{1,2,0:T(8,128)}) %all-gather.21.cloned.1.call-update) | async-done | bytes 1048592 | tf_op jit(solution)/shard_map/all_gather | solution.py:58
  288.9 11.7 %cholesky.358 = f32[128,128]{1,0:T(8,128)S(1)} custom-call(f32[128,128]{1,0:T(8,128)S(1)} %cholesky.439), custom_call_target="Cholesky" | custom-call | tf_op jit(solution)/shard_map/jit(cholesky)/cholesky | solution.py:59
  313.2 11.7 %cholesky.377 = f32[128,128]{1,0:T(8,128)S(1)} custom-call(f32[128,128]{1,0:T(8,128)S(1)} %cholesky.443), custom_call_target="Cholesky" | custom-call | tf_op jit(solution)/shard_map/jit(cholesky)/cholesky | solution.py:59
  326.2 9.9 %custom-call.34 = f32[1,128,128]{1,2,0:T(8,128)S(1)} custom-call(f32[1,128,128]{2,1,0:T(8,128)S(1)} %get-tuple-element.57), custom_call_target="InvertDiagBlocksLowerTriangular" | custom-call | tf_op jit(solution)/shard_map/jit(cholesky)/cholesky | solution.py:59
  337.7 11.7 %cholesky.398 = f32[128,128]{1,0:T(8,128)S(1)} custom-call(f32[128,128]{1,0:T(8,128)S(1)} %cholesky.448), custom_call_target="Cholesky" | custom-call | tf_op jit(solution)/shard_map/jit(cholesky)/cholesky | solution.py:59
  361.4 11.7 %cholesky.415 = f32[128,128]{1,0:T(8,128)S(1)} custom-call(f32[128,128]{1,0:T(8,128)S(1)} %convolution_subtract_fusion.13), custom_call_target="Cholesky" | custom-call | tf_op jit(solution)/shard_map/jit(cholesky)/cholesky | solution.py:59
  378.4 14.4 %while.5 = (s32[]{:T(128)}, f32[512,512]{1,0:T(8,128)}, s32[4,2]{0,1:T(2,128)S(1)}, f32[4,128,128]{2,1,0:T(8,128)}, s32[]{:T(128)}) while((s32[]{:T(128)}, f32[512,512]{1,0:T(8,128)}, s32[4,2]{0,1:T(2,128)S(1)}, f32[4,128,128]{2,1,0:T(8,128)}, s32[]{:T(128)}) %tuple.80), condition=%wide.while_cond.clone, body=%wide.while_body.clone.sunk | while | flops 2 | bytes 132705 | solution.py:33
  392.8 40.2 %custom-call.36 = f32[4,128,128]{1,2,0:T(8,128)S(1)} custom-call(f32[4,128,128]{2,1,0:T(8,128)} %get-tuple-element.20), custom_call_target="InvertDiagBlocksLowerTriangular" | custom-call | tf_op jit(solution)/shard_map/jit(_cho_solve)/triangular_solve | solution.py:33
  455.2 20.9 %collective-permute-done.4 = f32[512,512]{1,0:T(8,128)} collective-permute-done((f32[512,512]{1,0:T(8,128)S(1)}, f32[512,512]{1,0:T(8,128)}, u32[]{:S(2)}, u32[]{:S(2)}) %collective-permute-start.4) | collective-permute-done | bytes 1048608 | tf_op jit(solution)/shard_map/ppermute | solution.py:13
  479.8 16.5 %collective-permute-done.3 = f32[2,512,512]{2,1,0:T(8,128)} collective-permute-done((f32[2,512,512]{2,1,0:T(8,128)}, f32[2,512,512]{2,1,0:T(8,128)}, u32[]{:S(2)}, u32[]{:S(2)}) %collective-permute-start.3) | collective-permute-done | bytes 2097184 | tf_op jit(solution)/shard_map/ppermute | solution.py:13
  496.3 15.0 %all-gather.13.cloned.1.call-done = f32[512,512]{1,0:T(8,128)} async-done(((f32[512,128]{1,0:T(8,128)}), f32[512,512]{1,0:T(8,128)}) %all-gather.13.cloned.1.call-update) | async-done | bytes 1048592 | tf_op jit(solution)/shard_map/all_gather | solution.py:67
  522.8 41.0 %all-gather.19.cloned.1.call-done = f32[2,512,512]{1,2,0:T(8,128)} async-done(((f32[2,128,512]{1,2,0:T(8,128)}), f32[2,512,512]{1,2,0:T(8,128)}) %all-gather.19.cloned.1.call-update) | async-done | bytes 2097168 | tf_op jit(solution)/shard_map/all_gather | solution.py:89
  592.2 15.5 %collective-permute-done.8 = f32[2,128,512]{1,2,0:T(8,128)S(1)} collective-permute-done((f32[2,128,512]{1,2,0:T(8,128)S(1)}, f32[2,128,512]{1,2,0:T(8,128)S(1)}, u32[]{:S(2)}, u32[]{:S(2)}) %collective-permute-start.8) | collective-permute-done | bytes 524320 | tf_op jit(solution)/shard_map/ppermute | solution.py:13
  (218 shorter events, 197.7 us)
Async XLA Ops:
  9.1 104.2 %all-to-all-start = ((f32[4,128,128]{1,2,0:T(8,128)}), f32[4,128,128]{1,2,0:T(8,128)}, u32[]{:S(2)}, u32[]{:S(2)}) async-start(f32[4,128,128]{1,2,0:T(8,128)} %copy.9), calls=%async_computation | async-start | bytes 524288 | tf_op jit(solution)/shard_map/all_to_all | solution.py:45
  13.4 183.2 %all-gather.9.cloned.1.call-start = ((), (), s32[]{:S(2)}) async-start(), calls=%async_computation.1 | async-start | bytes 1310720 | tf_op jit(solution)/shard_map/all_gather | solution.py:67
  113.2 44.1 %collective-permute-start = (f32[128,512]{0,1:T(8,128)}, f32[128,512]{0,1:T(8,128)S(1)}, u32[]{:S(2)}, u32[]{:S(2)}) collective-permute-start(f32[128,512]{0,1:T(8,128)} %bitcast.13), channel_id=1, source_target_pairs={{4,0},{8,4},{12,8},{16,12},{20,16},{24,20},{28,24},{32,28},{36,32}... | collective-permute-start | bytes 786440 | tf_op jit(solution)/shard_map/ppermute | solution.py:13
  117.0 40.3 %copy-start.12 = (f32[512,128]{1,0:T(8,128)}, f32[512,128]{1,0:T(8,128)S(1)}, u32[]{:S(2)}) copy-start(f32[512,128]{1,0:T(8,128)S(1)} %fusion.50) | copy-start | bytes 786436
  163.3 33.2 %copy-start.15 = (f32[128,512]{0,1:T(8,128)S(1)}, f32[128,512]{0,1:T(8,128)}, u32[]{:S(2)}) copy-start(f32[128,512]{0,1:T(8,128)} %copy-done.14) | copy-start | bytes 786436
  164.6 66.9 %all-gather.11.cloned.1.call-start = ((), (), s32[]{:S(2)}) async-start(), calls=%async_computation.2 | async-start | bytes 1310720 | tf_op jit(solution)/shard_map/all_gather | solution.py:68
  165.4 118.5 %all-gather.21.cloned.1.call-start = ((), (), s32[]{:S(2)}) async-start(), calls=%async_computation.7 | async-start | bytes 1310720 | tf_op jit(solution)/shard_map/all_gather | solution.py:58
  202.4 36.9 %collective-permute-start.1 = (f32[2,128,512]{1,2,0:T(8,128)}, f32[2,128,512]{1,2,0:T(8,128)}, u32[]{:S(2)}, u32[]{:S(2)}) collective-permute-start(f32[2,128,512]{1,2,0:T(8,128)} %pad_maximum_fusion.4), channel_id=1, source_target_pairs={{4,0},{8,4},{12,8},{16,12},{20,16},{24,20},{28,24},{32,28},{36,32}... | collective-permute-start | bytes 1572872 | tf_op jit(solution)/shard_map/ppermute | solution.py:13
  237.4 14.1 %collective-permute-start.2 = (f32[2,128,512]{1,2,0:T(8,128)}, f32[2,128,512]{1,2,0:T(8,128)}, u32[]{:S(2)}, u32[]{:S(2)}) collective-permute-start(f32[2,128,512]{1,2,0:T(8,128)} %pad_maximum_fusion.5), channel_id=1, source_target_pairs={{0,4},{4,8},{8,12},{12,16},{16,20},{20,24},{24,28},{28,32},{32,36}... | collective-permute-start | bytes 1572872 | tf_op jit(solution)/shard_map/ppermute | solution.py:13
  239.3 17.7 %copy-start.13 = (f32[512,128]{1,0:T(8,128)S(1)}, f32[512,128]{1,0:T(8,128)}, u32[]{:S(2)}) copy-start(f32[512,128]{1,0:T(8,128)} %copy-done.12) | copy-start | bytes 786436
  253.6 190.7 %all-gather.15.cloned.1.call-start = ((), (), s32[]{:S(2)}) async-start(), calls=%async_computation.4 | async-start | bytes 2621440 | tf_op jit(solution)/shard_map/all_gather | solution.py:89
  256.5 220.1 %all-gather.17.cloned.1.call-start = ((), (), s32[]{:S(2)}) async-start(), calls=%async_computation.5 | async-start | bytes 1310720 | tf_op jit(solution)/shard_map/all_gather | solution.py:68
  392.8 44.9 %copy-start.5 = (f32[512,512]{1,0:T(8,128)S(1)}, f32[512,512]{1,0:T(8,128)}, u32[]{:S(2)}) copy-start(f32[512,512]{1,0:T(8,128)} %get-tuple-element.176) | copy-start | bytes 3145732
  444.2 67.2 %all-gather.13.cloned.1.call-start = ((), (), s32[]{:S(2)}) async-start(), calls=%async_computation.3 | async-start | bytes 1310720 | tf_op jit(solution)/shard_map/all_gather | solution.py:67
  444.3 52.0 %collective-permute-start.3 = (f32[2,512,512]{2,1,0:T(8,128)}, f32[2,512,512]{2,1,0:T(8,128)}, u32[]{:S(2)}, u32[]{:S(2)}) collective-permute-start(f32[2,512,512]{2,1,0:T(8,128)} %all-gather.15.cloned.1.call-done), channel_id=1, source_target_pairs={{0,8},{4,12},{8,16},{12,20},{16,24},{20,28},{24,32},{28,36},{32,40... | collective-permute-start | bytes 6291464 | tf_op jit(solution)/shard_map/ppermute | solution.py:13
  447.7 116.1 %all-gather.19.cloned.1.call-start = ((), (), s32[]{:S(2)}) async-start(), calls=%async_computation.6 | async-start | bytes 2621440 | tf_op jit(solution)/shard_map/all_gather | solution.py:89
  449.0 27.0 %collective-permute-start.4 = (f32[512,512]{1,0:T(8,128)S(1)}, f32[512,512]{1,0:T(8,128)}, u32[]{:S(2)}, u32[]{:S(2)}) collective-permute-start(f32[512,512]{1,0:T(8,128)S(1)} %slice_bitcast_fusion.4), channel_id=1, source_target_pairs={{8,0},{12,4},{16,8},{20,12},{24,16},{28,20},{32,24},{36,28},{40,32... | collective-permute-start | bytes 3145736 | tf_op jit(solution)/shard_map/ppermute | solution.py:13
  476.6 38.0 %copy-start.2 = (f32[512,512]{1,0:T(8,128)S(1)}, f32[512,512]{1,0:T(8,128)}, u32[]{:S(2)}) copy-start(f32[512,512]{1,0:T(8,128)} %all-gather.17.cloned.1.call-done) | copy-start | bytes 3145732
  563.8 48.1 %collective-permute-start.5 = (f32[2,512,512]{1,2,0:T(8,128)}, f32[2,512,512]{1,2,0:T(8,128)}, u32[]{:S(2)}, u32[]{:S(2)}) collective-permute-start(f32[2,512,512]{1,2,0:T(8,128)} %all-gather.19.cloned.1.call-done), channel_id=1, source_target_pairs={{0,4},{4,8},{8,12},{12,16},{16,20},{20,24},{24,28},{28,32},{32,36}... | collective-permute-start | bytes 6291464 | tf_op jit(solution)/shard_map/ppermute | solution.py:13
  569.0 11.3 %copy-start.19 = (f32[2,512,512]{1,2,0:T(8,128)S(1)}, f32[2,512,512]{1,2,0:T(8,128)}, u32[]{:S(2)}) copy-start(f32[2,512,512]{1,2,0:T(8,128)} %all-gather.19.cloned.1.call-done) | copy-start | bytes 6291460
  572.8 19.4 %collective-permute-start.7 = (f32[2,128,512]{1,2,0:T(8,128)}, f32[2,128,512]{1,2,0:T(8,128)}, u32[]{:S(2)}, u32[]{:S(2)}) collective-permute-start(f32[2,128,512]{1,2,0:T(8,128)} %pad_maximum_fusion.8), channel_id=1, source_target_pairs={{8,0},{12,4},{16,8},{20,12},{24,16},{28,20},{32,24},{36,28},{40,32... | collective-permute-start | bytes 1572872 | tf_op jit(solution)/shard_map/ppermute | solution.py:13
  580.3 27.4 %copy-start.11 = (f32[1,128,512]{1,2,0:T(8,128)S(1)}, f32[1,128,512]{1,2,0:T(8,128)}, u32[]{:S(2)}) copy-start(f32[1,128,512]{1,2,0:T(8,128)} %get-tuple-element.48) | copy-start | bytes 786436
  581.4 28.1 %collective-permute-start.6 = (f32[512,512]{0,1:T(8,128)}, f32[512,512]{0,1:T(8,128)}, u32[]{:S(2)}, u32[]{:S(2)}) collective-permute-start(f32[512,512]{0,1:T(8,128)} %slice_bitcast_fusion), channel_id=1, source_target_pairs={{4,0},{8,4},{12,8},{16,12},{20,16},{24,20},{28,24},{32,28},{36,32}... | collective-permute-start | bytes 3145736 | tf_op jit(solution)/shard_map/ppermute | solution.py:13
  588.6 19.2 %collective-permute-start.8 = (f32[2,128,512]{1,2,0:T(8,128)S(1)}, f32[2,128,512]{1,2,0:T(8,128)S(1)}, u32[]{:S(2)}, u32[]{:S(2)}) collective-permute-start(f32[2,128,512]{1,2,0:T(8,128)S(1)} %pad_maximum_fusion.9), channel_id=1, source_target_pairs={{0,8},{4,12},{8,16},{12,20},{16,24},{20,28},{24,32},{28,36},{32,40... | collective-permute-start | bytes 1572872 | tf_op jit(solution)/shard_map/ppermute | solution.py:13
  (13 other events, 37.8 us)
Sparse Core Ops, SparseCore 0:
  164.8 31.7 all-gather.8
  199.2 32.2 all-gather.10
  253.7 30.1 all-gather.20
  285.8 37.4 all-gather.14
  444.3 32.2 all-gather.16
  479.1 32.2 all-gather.12
  522.9 40.8 all-gather.18
where the time goes:
time: 641 us; the launch traced here: 630 us
  other arithmetic  259 us (40%)
  waiting for transfers between devices  206 us (32%)
  matrix products  70.9 us (11%)
  starting transfers between devices  38 us (6%)
  local copies, waits for them, and re-layouts  36.8 us (6%)
  between operations  20.4 us (3%)
    another operation x29, other arithmetic, local(): factor = jnp.linalg.cholesky(whole_pivot)  163 us
    another operation x7, other arithmetic, solve_with(): return jax.scipy.linalg.cho_solve((factor, True), right_side)  81 us
    ppermute x9, waiting for transfers between devices, passed_along(): lax.ppermute(value, axis, [(source, source + steps) for source in range(l...  65.1 us
    all_gather x2, waiting for transfers between devices, local(): lax.all_gather(left_columns, 'rows', axis=1, tiled=True)  46.2 us
    all_gather x2, waiting for transfers between devices, local(): lax.all_gather(jnp.stack([diagonal_rows, coupling_rows]), 'rows', axis=1,...  41 us
    ppermute x9, starting transfers between devices, passed_along(): lax.ppermute(value, axis, [(source, source + steps) for source in range(l...  33 us
    all_gather x2, waiting for transfers between devices, local(): lax.all_gather(right_columns, 'rows', axis=1, tiled=True)  26.5 us
    all_gather x1, waiting for transfers between devices, local(): whole_pivot = lax.all_gather(pivot_rows, 'rows', axis=0, tiled=True)  26 us
  transfers between devices with their start and end apart: 17, of which 10 were waited for; matrix products, arithmetic and copies ran while one was open for 52% of the time, Pallas kernels for 0%

commit v1 on v0

--- a/solution.py
+++ b/solution.py
@@ -5,6 +5,19 @@
 
 LEVELS = 2
 precise = lax.Precision.HIGHEST
+
+
+def gather_around(x, axis, dim):
+    ways = lax.axis_size(axis)
+    up = [(d, (d + 1) % ways) for d in range(ways)]
+    down = [(d, (d - 1) % ways) for d in range(ways)]
+    earlier, later = ([x], [x])
+    for _ in range(ways // 2):
+        earlier.append(lax.ppermute(earlier[-1], axis, up))
+    for _ in range((ways - 1) // 2):
+        later.append(lax.ppermute(later[-1], axis, down))
+    line = jnp.concatenate([*earlier[::-1], *later[1:]], axis=dim)
+    return jnp.roll(line, (lax.axis_index(axis) - ways // 2) * x.shape[dim], axis=dim)
 
 
 def passed_along(value, axis, steps):
@@ -64,7 +77,7 @@
         right_columns = solved[:, quarter : 2 * quarter]
         inverse_columns = solved[:, 2 * quarter :]
         left_solved, right_solved = (
-            lax.all_gather(left_columns, "rows", axis=1, tiled=True),
+            gather_around(left_columns, "rows", 1),
             lax.all_gather(right_columns, "rows", axis=1, tiled=True),
         )
         drop_left = product_over(lower_columns, left_solved)

time: 641 us -> 600 us (0.936)
  waiting for transfers between devices: 206 us -> 146 us
  starting transfers between devices: 38 us -> 53.9 us
    all_gather x2 -> x0, waiting for transfers between devices: 46.2 us -> none  [local(): lax.all_gather(left_columns, 'rows', axis=1, tiled=True)]
    ppermute x9, waiting for transfers between devices: 65.1 us -> 28 us  [passed_along(): lax.ppermute(value, axis, [(source, source + steps) for source in range(l...]
    ppermute x0 -> x6, waiting for transfers between devices: none -> 27.8 us  [the longest x4 26.7 us: gather_around(): earlier.append(lax.ppermute(earlier[-1], axis, up))]
    all_gather x2, waiting for transfers between devices: 26.5 us -> 4.3 us  [local(): lax.all_gather(right_columns, 'rows', axis=1, tiled=True)]
    ppermute x0 -> x6, starting transfers between devices: none -> 18.8 us  [the longest x4 11 us: gather_around(): earlier.append(lax.ppermute(earlier[-1], axis, up))]
    all_gather x2, waiting for transfers between devices: 41 us -> 55.9 us  [local(): lax.all_gather(jnp.stack([diagonal_rows, coupling_rows]), 'rows', axis=1,...]
  transfers between devices with their start and end apart: 17 -> 21, of which waited for: 10 -> 12; matrix products, arithmetic and copies ran while one was open for 52% -> 57% of each run, Pallas kernels for 0% -> 0%
where the time goes in v1:
time: 600 us; the launch traced here: 589 us
  other arithmetic  262 us (44%)
  waiting for transfers between devices  146 us (24%)
  matrix products  71.7 us (12%)
  starting transfers between devices  53.9 us (9%)
  local copies, waits for them, and re-layouts  35 us (6%)
  between operations  20.3 us (3%)
    another operation x29, other arithmetic, local(): factor = jnp.linalg.cholesky(whole_pivot)  160 us
    another operation x7, other arithmetic, solve_with(): return jax.scipy.linalg.cho_solve((factor, True), right_side)  82.2 us
    all_gather x2, waiting for transfers between devices, local(): lax.all_gather(jnp.stack([diagonal_rows, coupling_rows]), 'rows', axis=1,...  55.9 us
    ppermute x9, starting transfers between devices, passed_along(): lax.ppermute(value, axis, [(source, source + steps) for source in range(l...  30.6 us
    all_gather x1, waiting for transfers between devices, local(): whole_pivot = lax.all_gather(pivot_rows, 'rows', axis=0, tiled=True)  30.2 us
    ppermute x9, waiting for transfers between devices, passed_along(): lax.ppermute(value, axis, [(source, source + steps) for source in range(l...  28 us
    ppermute x4, waiting for transfers between devices, gather_around(): earlier.append(lax.ppermute(earlier[-1], axis, up))  26.7 us
    dot_general x8, matrix products, product_over(): lax.dot_general(left, right, (((0,), (0,)), ((), ())), precision=precise,...  21.4 us
  transfers between devices with their start and end apart: 21, of which 12 were waited for; matrix products, arithmetic and copies ran while one was open for 57% of the time, Pallas kernels for 0%

profile of v1, /device:TPU:256, one launch (start us, length us, event | category | flops | bytes accessed | tf_op | source)
XLA Modules:
  0.0 589.2 jit_solution(10296251054372047777)
XLA Ops:
  14.0 11.7 %cholesky.286 = f32[128,128]{1,0:T(8,128)S(1)} custom-call(f32[128,128]{1,0:T(8,128)S(1)} %cholesky.426), custom_call_target="Cholesky" | custom-call | tf_op jit(solution)/shard_map/jit(cholesky)/cholesky | solution.py:72
  25.7 9.8 %custom-call.29 = f32[1,128,128]{1,2,0:T(8,128)S(1)} custom-call(f32[1,128,128]{2,1,0:T(8,128)S(1)} %get-tuple-element.71), custom_call_target="InvertDiagBlocksLowerTriangular" | custom-call | tf_op jit(solution)/shard_map/jit(cholesky)/cholesky | solution.py:72
  36.3 11.7 %cholesky.305 = f32[128,128]{1,0:T(8,128)S(1)} custom-call(f32[128,128]{1,0:T(8,128)S(1)} %cholesky.430), custom_call_target="Cholesky" | custom-call | tf_op jit(solution)/shard_map/jit(cholesky)/cholesky | solution.py:72
  48.1 10.2 %custom-call.30 = f32[1,128,128]{1,2,0:T(8,128)S(1)} custom-call(f32[1,128,128]{2,1,0:T(8,128)S(1)} %get-tuple-element.68), custom_call_target="InvertDiagBlocksLowerTriangular" | custom-call | tf_op jit(solution)/shard_map/jit(cholesky)/cholesky | solution.py:72
  59.0 11.7 %cholesky.326 = f32[128,128]{1,0:T(8,128)S(1)} custom-call(f32[128,128]{1,0:T(8,128)S(1)} %cholesky.435), custom_call_target="Cholesky" | custom-call | tf_op jit(solution)/shard_map/jit(cholesky)/cholesky | solution.py:72
  71.5 9.8 %custom-call.31 = f32[1,128,128]{1,2,0:T(8,128)S(1)} custom-call(f32[1,128,128]{2,1,0:T(8,128)S(1)} %get-tuple-element.65), custom_call_target="InvertDiagBlocksLowerTriangular" | custom-call | tf_op jit(solution)/shard_map/jit(cholesky)/cholesky | solution.py:72
  81.9 11.7 %cholesky.343 = f32[128,128]{1,0:T(8,128)S(1)} custom-call(f32[128,128]{1,0:T(8,128)S(1)} %convolution_subtract_fusion.14), custom_call_target="Cholesky" | custom-call | tf_op jit(solution)/shard_map/jit(cholesky)/cholesky | solution.py:72
  110.1 39.3 %custom-call.32 = f32[4,128,128]{1,2,0:T(8,128)S(1)} custom-call(f32[4,128,128]{2,1,0:T(8,128)S(1)} %get-tuple-element.20), custom_call_target="InvertDiagBlocksLowerTriangular" | custom-call | tf_op jit(solution)/shard_map/jit(_cho_solve)/triangular_solve | solution.py:46
  170.7 9.6 %collective-permute-done.2 = f32[512,128]{1,0:T(8,128)} collective-permute-done((f32[512,128]{1,0:T(8,128)S(1)}, f32[512,128]{1,0:T(8,128)}, u32[]{:S(2)}, u32[]{:S(2)}) %collective-permute-start.2) | collective-permute-done | bytes 262176 | tf_op jit(solution)/shard_map/ppermute | solution.py:16
  199.3 12.2 %collective-permute-done.5 = f32[2,128,512]{1,2,0:T(8,128)} collective-permute-done((f32[2,128,512]{1,2,0:T(8,128)}, f32[2,128,512]{1,2,0:T(8,128)}, u32[]{:S(2)}, u32[]{:S(2)}) %collective-permute-start.5) | collective-permute-done | bytes 524320 | tf_op jit(solution)/shard_map/ppermute | solution.py:26
  215.8 15.5 %all-gather.9.cloned.1.call-done = f32[2,512,512]{2,1,0:T(8,128)} async-done(((f32[2,128,512]{2,1,0:T(8,128)}), f32[2,512,512]{2,1,0:T(8,128)}) %all-gather.9.cloned.1.call-update) | async-done | bytes 2097168 | tf_op jit(solution)/shard_map/all_gather | solution.py:102
  235.1 30.2 %all-gather.15.cloned.1.call-done = f32[1,512,512]{1,2,0:T(8,128)} async-done(((f32[1,128,512]{1,2,0:T(8,128)}), f32[1,512,512]{1,2,0:T(8,128)}) %all-gather.15.cloned.1.call-update) | async-done | bytes 1048592 | tf_op jit(solution)/shard_map/all_gather | solution.py:71
  270.6 11.7 %cholesky.358 = f32[128,128]{1,0:T(8,128)S(1)} custom-call(f32[128,128]{1,0:T(8,128)S(1)} %cholesky.439), custom_call_target="Cholesky" | custom-call | tf_op jit(solution)/shard_map/jit(cholesky)/cholesky | solution.py:72
  282.9 9.8 %custom-call.33 = f32[1,128,128]{1,2,0:T(8,128)S(1)} custom-call(f32[1,128,128]{2,1,0:T(8,128)S(1)} %get-tuple-element.61), custom_call_target="InvertDiagBlocksLowerTriangular" | custom-call | tf_op jit(solution)/shard_map/jit(cholesky)/cholesky | solution.py:72
  297.1 11.7 %cholesky.377 = f32[128,128]{1,0:T(8,128)S(1)} custom-call(f32[128,128]{1,0:T(8,128)S(1)} %cholesky.443), custom_call_target="Cholesky" | custom-call | tf_op jit(solution)/shard_map/jit(cholesky)/cholesky | solution.py:72
  310.1 9.9 %custom-call.34 = f32[1,128,128]{1,2,0:T(8,128)S(1)} custom-call(f32[1,128,128]{2,1,0:T(8,128)S(1)} %get-tuple-element.58), custom_call_target="InvertDiagBlocksLowerTriangular" | custom-call | tf_op jit(solution)/shard_map/jit(cholesky)/cholesky | solution.py:72
  322.5 11.7 %cholesky.398 = f32[128,128]{1,0:T(8,128)S(1)} custom-call(f32[128,128]{1,0:T(8,128)S(1)} %cholesky.448), custom_call_target="Cholesky" | custom-call | tf_op jit(solution)/shard_map/jit(cholesky)/cholesky | solution.py:72
  335.5 9.8 %custom-call.35 = f32[1,128,128]{1,2,0:T(8,128)S(1)} custom-call(f32[1,128,128]{2,1,0:T(8,128)S(1)} %get-tuple-element.55), custom_call_target="InvertDiagBlocksLowerTriangular" | custom-call | tf_op jit(solution)/shard_map/jit(cholesky)/cholesky | solution.py:72
  347.5 11.7 %cholesky.415 = f32[128,128]{1,0:T(8,128)S(1)} custom-call(f32[128,128]{1,0:T(8,128)S(1)} %convolution_subtract_fusion.13), custom_call_target="Cholesky" | custom-call | tf_op jit(solution)/shard_map/jit(cholesky)/cholesky | solution.py:72
  365.6 11.6 %while.5 = (s32[]{:T(128)}, f32[512,512]{1,0:T(8,128)}, s32[4,2]{0,1:T(2,128)S(1)}, f32[4,128,128]{2,1,0:T(8,128)S(1)}, s32[]{:T(128)}) while((s32[]{:T(128)}, f32[512,512]{1,0:T(8,128)}, s32[4,2]{0,1:T(2,128)S(1)}, f32[4,128,128]{2,1,0:T(8,128)S(1)}, s32[]{:T(128)}) %tuple.77), condition=%wide.while_cond.clone, body=%wide.while_body.clone.sunk | while | flops 2 | bytes 131189 | solution.py:46
  377.9 40.1 %custom-call.36 = f32[4,128,128]{1,2,0:T(8,128)S(1)} custom-call(f32[4,128,128]{2,1,0:T(8,128)} %copy-done.16), custom_call_target="InvertDiagBlocksLowerTriangular" | custom-call | tf_op jit(solution)/shard_map/jit(_cho_solve)/triangular_solve | solution.py:46
  449.6 10.8 %collective-permute-done.7 = f32[512,128]{1,0:T(8,128)} collective-permute-done((f32[512,128]{1,0:T(8,128)}, f32[512,128]{1,0:T(8,128)}, u32[]{:S(2)}, u32[]{:S(2)}) %collective-permute-start.7) | collective-permute-done | bytes 262176 | tf_op jit(solution)/shard_map/ppermute | solution.py:16
  479.6 40.4 %all-gather.13.cloned.1.call-done = f32[2,512,512]{1,2,0:T(8,128)} async-done(((f32[2,128,512]{1,2,0:T(8,128)}), f32[2,512,512]{1,2,0:T(8,128)}) %all-gather.13.cloned.1.call-update) | async-done | bytes 2097168 | tf_op jit(solution)/shard_map/all_gather | solution.py:102
  549.4 15.8 %collective-permute-done.14 = f32[2,128,512]{1,2,0:T(8,128)} collective-permute-done((f32[2,128,512]{1,2,0:T(8,128)}, f32[2,128,512]{1,2,0:T(8,128)}, u32[]{:S(2)}, u32[]{:S(2)}) %collective-permute-start.14) | collective-permute-done | bytes 524320 | tf_op jit(solution)/shard_map/ppermute | solution.py:26
  (222 shorter events, 210.1 us)
Async XLA Ops:
  9.1 97.2 %all-to-all-start = ((f32[4,128,128]{1,2,0:T(8,128)}), f32[4,128,128]{1,2,0:T(8,128)}, u32[]{:S(2)}, u32[]{:S(2)}) async-start(f32[4,128,128]{1,2,0:T(8,128)} %copy.9), calls=%async_computation | async-start | bytes 524288 | tf_op jit(solution)/shard_map/all_to_all | solution.py:58
  13.4 177.3 %all-gather.7.cloned.1.call-start = ((), (), s32[]{:S(2)}) async-start(), calls=%async_computation.1 | async-start | bytes 1310720 | tf_op jit(solution)/shard_map/all_gather | solution.py:81
  106.3 44.1 %collective-permute-start = (f32[128,512]{0,1:T(8,128)}, f32[128,512]{0,1:T(8,128)S(1)}, u32[]{:S(2)}, u32[]{:S(2)}) collective-permute-start(f32[128,512]{0,1:T(8,128)} %bitcast.13), channel_id=1, source_target_pairs={{4,0},{8,4},{12,8},{16,12},{20,16},{24,20},{28,24},{32,28},{36,32}... | collective-permute-start | bytes 786440 | tf_op jit(solution)/shard_map/ppermute | solution.py:26
  110.0 40.3 %copy-start.11 = (f32[512,128]{1,0:T(8,128)}, f32[512,128]{1,0:T(8,128)S(1)}, u32[]{:S(2)}) copy-start(f32[512,128]{1,0:T(8,128)S(1)} %fusion.58) | copy-start | bytes 786436
  150.4 33.0 %copy-start.13 = (f32[128,512]{0,1:T(8,128)}, f32[128,512]{0,1:T(8,128)S(1)}, u32[]{:S(2)}) copy-start(f32[128,512]{0,1:T(8,128)S(1)} %collective-permute-done) | copy-start | bytes 786436
  156.9 74.4 %all-gather.9.cloned.1.call-start = ((), (), s32[]{:S(2)}) async-start(), calls=%async_computation.2 | async-start | bytes 2621440 | tf_op jit(solution)/shard_map/all_gather | solution.py:102
  157.9 107.4 %all-gather.15.cloned.1.call-start = ((), (), s32[]{:S(2)}) async-start(), calls=%async_computation.5 | async-start | bytes 1310720 | tf_op jit(solution)/shard_map/all_gather | solution.py:71
  157.9 10.3 %collective-permute-start.1 = (f32[512,128]{1,0:T(8,128)S(1)}, f32[512,128]{1,0:T(8,128)S(1)}, u32[]{:S(2)}, u32[]{:S(2)}) collective-permute-start(f32[512,128]{1,0:T(8,128)S(1)} %get-tuple-element.48), channel_id=1, source_target_pairs={{0,1},{1,2},{2,3},{3,0},{4,5},{5,6},{6,7},{7,4},{8,9},{9,10},{10,1... | collective-permute-start | bytes 786440 | tf_op jit(solution)/shard_map/ppermute | solution.py:16
  161.5 9.2 %collective-permute-start.3 = (f32[512,128]{1,0:T(8,128)S(1)}, f32[512,128]{1,0:T(8,128)S(1)}, u32[]{:S(2)}, u32[]{:S(2)}) collective-permute-start(f32[512,128]{1,0:T(8,128)S(1)} %get-tuple-element.48), channel_id=1, source_target_pairs={{0,3},{1,0},{2,1},{3,2},{4,7},{5,4},{6,5},{7,6},{8,11},{9,8},{10,9... | collective-permute-start | bytes 786440 | tf_op jit(solution)/shard_map/ppermute | solution.py:18
  168.2 12.1 %collective-permute-start.2 = (f32[512,128]{1,0:T(8,128)S(1)}, f32[512,128]{1,0:T(8,128)}, u32[]{:S(2)}, u32[]{:S(2)}) collective-permute-start(f32[512,128]{1,0:T(8,128)S(1)} %collective-permute-done.1), channel_id=1, source_target_pairs={{0,1},{1,2},{2,3},{3,0},{4,5},{5,6},{6,7},{7,4},{8,9},{9,10},{10,1... | collective-permute-start | bytes 786440 | tf_op jit(solution)/shard_map/ppermute | solution.py:16
  186.0 13.3 %collective-permute-start.4 = (f32[2,128,512]{1,2,0:T(8,128)}, f32[2,128,512]{1,2,0:T(8,128)}, u32[]{:S(2)}, u32[]{:S(2)}) collective-permute-start(f32[2,128,512]{1,2,0:T(8,128)} %pad_maximum_fusion.4), channel_id=1, source_target_pairs={{4,0},{8,4},{12,8},{16,12},{20,16},{24,20},{28,24},{32,28},{36,32}... | collective-permute-start | bytes 1572872 | tf_op jit(solution)/shard_map/ppermute | solution.py:26
  197.4 14.1 %collective-permute-start.5 = (f32[2,128,512]{1,2,0:T(8,128)}, f32[2,128,512]{1,2,0:T(8,128)}, u32[]{:S(2)}, u32[]{:S(2)}) collective-permute-start(f32[2,128,512]{1,2,0:T(8,128)} %pad_maximum_fusion.5), channel_id=1, source_target_pairs={{0,4},{4,8},{8,12},{12,16},{16,20},{20,24},{24,28},{28,32},{32,36}... | collective-permute-start | bytes 1572872 | tf_op jit(solution)/shard_map/ppermute | solution.py:26
  213.7 251.2 %all-gather.11.cloned.1.call-start = ((), (), s32[]{:S(2)}) async-start(), calls=%async_computation.3 | async-start | bytes 1310720 | tf_op jit(solution)/shard_map/all_gather | solution.py:81
  231.3 236.9 %collective-permute-start.9 = (f32[2,512,512]{2,1,0:T(8,128)}, f32[2,512,512]{2,1,0:T(8,128)}, u32[]{:S(2)}, u32[]{:S(2)}) collective-permute-start(f32[2,512,512]{2,1,0:T(8,128)} %all-gather.9.cloned.1.call-done), channel_id=1, source_target_pairs={{0,8},{4,12},{8,16},{12,20},{16,24},{20,28},{24,32},{28,36},{32,40... | collective-permute-start | bytes 6291464 | tf_op jit(solution)/shard_map/ppermute | solution.py:26
  429.2 90.8 %all-gather.13.cloned.1.call-start = ((), (), s32[]{:S(2)}) async-start(), calls=%async_computation.4 | async-start | bytes 2621440 | tf_op jit(solution)/shard_map/all_gather | solution.py:102
  431.6 31.7 %collective-permute-start.10 = (f32[512,512]{1,0:T(8,128)}, f32[512,512]{1,0:T(8,128)}, u32[]{:S(2)}, u32[]{:S(2)}) collective-permute-start(f32[512,512]{1,0:T(8,128)} %slice_bitcast_fusion.4), channel_id=1, source_target_pairs={{8,0},{12,4},{16,8},{20,12},{24,16},{28,20},{32,24},{36,28},{40,32... | collective-permute-start | bytes 3145736 | tf_op jit(solution)/shard_map/ppermute | solution.py:26
  436.1 10.1 %collective-permute-start.6 = (f32[512,128]{1,0:T(8,128)S(1)}, f32[512,128]{1,0:T(8,128)}, u32[]{:S(2)}, u32[]{:S(2)}) collective-permute-start(f32[512,128]{1,0:T(8,128)S(1)} %get-tuple-element.45), channel_id=1, source_target_pairs={{0,1},{1,2},{2,3},{3,0},{4,5},{5,6},{6,7},{7,4},{8,9},{9,10},{10,1... | collective-permute-start | bytes 786440 | tf_op jit(solution)/shard_map/ppermute | solution.py:16
  438.8 10.8 %collective-permute-start.8 = (f32[512,128]{1,0:T(8,128)S(1)}, f32[512,128]{1,0:T(8,128)}, u32[]{:S(2)}, u32[]{:S(2)}) collective-permute-start(f32[512,128]{1,0:T(8,128)S(1)} %get-tuple-element.45), channel_id=1, source_target_pairs={{0,3},{1,0},{2,1},{3,2},{4,7},{5,4},{6,5},{7,6},{8,11},{9,8},{10,9... | collective-permute-start | bytes 786440 | tf_op jit(solution)/shard_map/ppermute | solution.py:18
  446.2 14.2 %collective-permute-start.7 = (f32[512,128]{1,0:T(8,128)}, f32[512,128]{1,0:T(8,128)}, u32[]{:S(2)}, u32[]{:S(2)}) collective-permute-start(f32[512,128]{1,0:T(8,128)} %collective-permute-done.6), channel_id=1, source_target_pairs={{0,1},{1,2},{2,3},{3,0},{4,5},{5,6},{6,7},{7,4},{8,9},{9,10},{10,1... | collective-permute-start | bytes 786440 | tf_op jit(solution)/shard_map/ppermute | solution.py:16
  520.0 51.2 %collective-permute-start.11 = (f32[2,512,512]{1,2,0:T(8,128)}, f32[2,512,512]{1,2,0:T(8,128)}, u32[]{:S(2)}, u32[]{:S(2)}) collective-permute-start(f32[2,512,512]{1,2,0:T(8,128)} %all-gather.13.cloned.1.call-done), channel_id=1, source_target_pairs={{0,4},{4,8},{8,12},{12,16},{16,20},{20,24},{24,28},{28,32},{32,36}... | collective-permute-start | bytes 6291464 | tf_op jit(solution)/shard_map/ppermute | solution.py:26
  529.3 20.1 %collective-permute-start.13 = (f32[2,128,512]{1,2,0:T(8,128)}, f32[2,128,512]{1,2,0:T(8,128)}, u32[]{:S(2)}, u32[]{:S(2)}) collective-permute-start(f32[2,128,512]{1,2,0:T(8,128)} %pad_maximum_fusion.8), channel_id=1, source_target_pairs={{8,0},{12,4},{16,8},{20,12},{24,16},{28,20},{32,24},{36,28},{40,32... | collective-permute-start | bytes 1572872 | tf_op jit(solution)/shard_map/ppermute | solution.py:26
  536.8 28.5 %copy-start.10 = (f32[1,128,512]{1,2,0:T(8,128)S(1)}, f32[1,128,512]{1,2,0:T(8,128)}, u32[]{:S(2)}) copy-start(f32[1,128,512]{1,2,0:T(8,128)} %get-tuple-element.49) | copy-start | bytes 786436
  537.9 30.9 %collective-permute-start.12 = (f32[512,512]{0,1:T(8,128)}, f32[512,512]{0,1:T(8,128)}, u32[]{:S(2)}, u32[]{:S(2)}) collective-permute-start(f32[512,512]{0,1:T(8,128)} %slice_bitcast_fusion), channel_id=1, source_target_pairs={{4,0},{8,4},{12,8},{16,12},{20,16},{24,20},{28,24},{32,28},{36,32}... | collective-permute-start | bytes 3145736 | tf_op jit(solution)/shard_map/ppermute | solution.py:26
  545.8 19.5 %collective-permute-start.14 = (f32[2,128,512]{1,2,0:T(8,128)}, f32[2,128,512]{1,2,0:T(8,128)}, u32[]{:S(2)}, u32[]{:S(2)}) collective-permute-start(f32[2,128,512]{1,2,0:T(8,128)} %pad_maximum_fusion.9), channel_id=1, source_target_pairs={{0,8},{4,12},{8,16},{12,20},{16,24},{20,28},{24,32},{28,36},{32,40... | collective-permute-start | bytes 1572872 | tf_op jit(solution)/shard_map/ppermute | solution.py:26
  (15 other events, 99.4 us)
Sparse Core Ops, SparseCore 0:
  157.0 33.5 all-gather.6
  192.7 38.4 all-gather.8
  233.9 31.2 all-gather.14
  429.3 35.5 all-gather.10
  479.8 40.1 all-gather.12
